TPU v7x, 256 devices: a whole 4x4x8 slice. The times are simulated.
256 devices in a mesh: dp: 16 (over y, z_hi), vocab: 16 (over x, z_lo, core).
Axes of the slice: x: 4, y: 4, z: 8 (z_hi: 4, z_lo: 2; z = z_hi * 2 + z_lo), core: 2. Of those that a mesh axis runs over, the one named last changes fastest.
Arguments:
- teacher_rows: bfloat16 [512, 4608], P('dp', 'vocab'), may hold values from -40 to 40
- student_rows: bfloat16 [512, 3584], P('dp', 'vocab'), may hold values from -40 to 40
- teacher_gain: bfloat16 [4608], P('vocab'), may hold values from 0.099609375 to 1.8984375
- student_gain: bfloat16 [3584], P('vocab'), may hold values from 0.099609375 to 1.8984375
- teacher_head: bfloat16 [4608, 131072], P(None, ('dp', 'vocab')), may hold values from -0.25 to 0.25
- student_head: bfloat16 [3584, 131072], P(None, ('dp', 'vocab')), may hold values from -0.3125 to 0.3125
- labels: int32 [512], replicated, may hold values from 0 to 131071
Outputs:
- mean_loss: float32 [], replicated
- head_grad: bfloat16 [3584, 131072], P(None, ('dp', 'vocab'))
- gain_grad: float32 [3584], P('vocab')
- rows_grad: float32 [512, 3584], P('dp', 'vocab')
All inputs are finite; a program needn't handle non-finite values.
Results may differ from a plain program's by a relative error of at most 0.0074.
Values may be sent and summed in bfloat16 or wider, within the bound.
A program may use at most 128 MiB of HBM per device.

v0:
```python
import functools

import jax
import jax.numpy as jnp
from jax import lax
from jax.experimental import pallas as pl
from jax.experimental.pallas import tpu as pltpu
from jax.sharding import PartitionSpec as P

MESH = pl.DeviceIdType.MESH
F32 = jnp.float32
BF16 = jnp.bfloat16
DT = 4608
DS = 3584
TOKENS = 512
CAP = 30.0
SCALE = 4096.0
EPS = 1e-06
WT = 288
WS = 224
NSEM = 160


def row_iota(shape):
    return lax.broadcasted_iota(jnp.int32, shape, 0)


def lane_iota(shape):
    return lax.broadcasted_iota(jnp.int32, shape, 1)


def kernel(
    tr, sr, tg, sg, lab, th, sh,
    loss_o, gain_o, rows_o, hg_o,
    G, TA, TB, SP, SPT, accT, accS, accA, NT, NS, gl, accZ,
    AT, AS, INVT, INVS, ST, LAB, SQ,
    MZ, MC, MX, MY, TC, TX, TY, TZ,
    PS, PR, R, RH, RB, Q, QR, W, ZR, NG,
    GI, GX, GXR, GY, GZ, GT,
    hsem, ssem, rsem,
):
    dp = lax.axis_index("dp")
    vo = lax.axis_index("vocab")
    y, zh = dp // 4, dp % 4
    x, zl, c = vo // 4, (vo // 2) % 2, vo % 2
    z = zh * 2 + zl
    zz = zl * 4 + zh
    pc = 1 - c

    def dev(x_, y_, z_, c_):
        return (y_ * 4 + z_ // 2, x_ * 4 + (z_ % 2) * 2 + c_)

    def m4(v):
        return lax.rem(v + 8, 4)

    def m8(v):
        return lax.rem(v + 16, 8)

    def at_x(d):
        return dev(m4(x + d), y, z, c)

    def at_y(d):
        return dev(x, m4(y + d), z, c)

    def at_z(d):
        return dev(x, y, m8(z + d), c)

    partner = dev(x, y, z, pc)

    def zidx(z_):
        return (z_ % 2) * 4 + z_ // 2

    count = [0]
    sent = []

    def send(src, dst, device):
        n = count[0]
        count[0] += 1
        cp = pltpu.make_async_remote_copy(
            src_ref=src, dst_ref=dst, send_sem=ssem.at[n], recv_sem=rsem.at[n],
            device_id=device, device_id_type=MESH,
        )
        cp.start()
        sent.append(cp)
        return n

    def recv(n, landing):
        pltpu.make_async_remote_copy(
            src_ref=landing, dst_ref=landing, send_sem=ssem.at[n], recv_sem=rsem.at[n],
            device_id=partner, device_id_type=MESH,
        ).wait_recv()

    def head_copies(v):
        v = jnp.int32(v)
        return (
            pltpu.make_async_copy(th.at[pl.ds(pl.multiple_of(v * WT, 16), 256)], TA.at[v], hsem.at[0, v]),
            pltpu.make_async_copy(th.at[pl.ds(pl.multiple_of(v * WT + 256, 16), 32)], TB.at[v, pl.ds(0, 32)], hsem.at[1, v]),
            pltpu.make_async_copy(sh.at[pl.ds(pl.multiple_of(v * WS, 16), WS)], SP.at[v, pl.ds(32, WS)], hsem.at[2, v]),
        )

    def wait_heads(v, _):
        for cp in head_copies(v):
            cp.wait()
        return 0

    barrier = pltpu.get_barrier_semaphore()
    others = [partner] + [at_x(d) for d in (1, 2, 3)] + [at_y(d) for d in (1, 2, 3)] + [at_z(d) for d in range(1, 8)]
    for d in others:
        pl.semaphore_signal(barrier, inc=1, device_id=d, device_id_type=MESH)

    AT[...] = jnp.zeros_like(AT)
    AS[...] = jnp.zeros_like(AS)
    AT[0:32, 0:WT] = tr[...].astype(F32)
    AS[0:32, 0:WS] = sr[...].astype(F32)
    AT[32:40, 0:WT] = jnp.broadcast_to(tg[...].astype(F32).reshape(1, WT), (8, WT))
    AS[32:40, 0:WS] = jnp.broadcast_to(sg[...].astype(F32).reshape(1, WS), (8, WS))
    a_t = AT[...]
    a_s = pltpu.roll(AS[...], 32, 1)
    AS[...] = a_s
    tiles = [a_t[:, 0:128], a_t[:, 128:256], a_t[:, 256:384] + a_s[:, 0:128], a_s[:, 128:256]]
    for j in range(4):
        b, o = (x, y) if j < 2 else (y, x)
        G[j, b, c, o, zz] = tiles[j][0:32].astype(BF16)
    sq_t = jnp.sum(a_t[0:32] * a_t[0:32], axis=1, keepdims=True)
    sq_s = jnp.sum(a_s[0:32] * a_s[0:32], axis=1, keepdims=True)
    sub, lane = row_iota((32, 128)), lane_iota((32, 128))
    MZ[zz] = jnp.zeros((8, 128), F32)
    MZ[zz, 0:1] = jnp.sum(jnp.where(lane == sub, sq_t, 0.0) + jnp.where(lane == sub + 32, sq_s, 0.0), axis=0, keepdims=True)
    for j in range(4):
        MZ[zz, 4 + j : 5 + j] = tiles[j][32:33]

    pl.semaphore_wait(barrier, len(others))

    mz = [send(MZ.at[zz], MZ.at[zz], at_z(d)) for d in range(1, 8)]
    zs = {}
    for j in (0, 2, 1, 3):
        b, o = (x, y) if j < 2 else (y, x)
        piece = G.at[j, b, c, o, zz]
        zs[j] = [send(piece, piece, at_z(d)) for d in range(1, 8)]

    def start_heads(v, _):
        for cp in head_copies(v):
            cp.start()
        return 0

    lax.fori_loop(0, 16, start_heads, 0)
    TB[:, 32:128, :] = jnp.zeros((16, 96, 512), BF16)
    SP[:, 0:32, :] = jnp.zeros((16, 32, 512), BF16)
    accT[...] = jnp.zeros_like(accT)
    accS[...] = jnp.zeros_like(accS)

    def axes(j):
        return (x, y, at_x, at_y) if j < 2 else (y, x, at_y, at_x)

    o1, o2, b1, b2, ds = {}, {}, {}, {}, {}

    def z_done(j):
        b, o, at_b, at_o = axes(j)
        for d in range(1, 8):
            recv(zs[j][d - 1], G.at[j, b, c, o, zidx(m8(z - d))])
        block = G.at[j, b, c, o]
        if j in (0, 2):
            o1[j] = [send(block, block, at_o(d)) for d in (1, 2, 3)]
        else:
            o1[j] = [send(block, block, at_o(1)), send(block, block, at_o(-1))]

    def o_near(j):
        b, o, at_b, at_o = axes(j)
        recv(o1[j][0], G.at[j, b, c, m4(o - 1)])
        half = G.at[j, b, c, m4(o - 1), pl.ds(0, 4)]
        f0 = send(half, half, at_o(1))
        recv(o1[j][1], G.at[j, b, c, m4(o + 1)])
        half = G.at[j, b, c, m4(o + 1), pl.ds(4, 4)]
        o2[j] = [f0, send(half, half, at_o(-1))]

    def o_far(j):
        b, o, at_b, at_o = axes(j)
        if j in (0, 2):
            for d in (1, 2, 3):
                recv(o1[j][d - 1], G.at[j, b, c, m4(o - d)])
        else:
            recv(o2[j][0], G.at[j, b, c, m4(o + 2), pl.ds(0, 4)])
            recv(o2[j][1], G.at[j, b, c, m4(o + 2), pl.ds(4, 4)])
        block = G.at[j, b, c]
        b1[j] = [send(block, block, at_b(1)), send(block, block, at_b(-1))]
        ds[j] = [send(block, block, partner)]

    def b_near(j):
        b, o, at_b, at_o = axes(j)
        recv(b1[j][0], G.at[j, m4(b - 1), c])
        half = G.at[j, m4(b - 1), c, pl.ds(0, 2)]
        f0 = send(half, half, at_b(1))
        recv(b1[j][1], G.at[j, m4(b + 1), c])
        half = G.at[j, m4(b + 1), c, pl.ds(2, 2)]
        b2[j] = [f0, send(half, half, at_b(-1))]
        for e in (-1, 1):
            block = G.at[j, m4(b + e), c]
            ds[j].append(send(block, block, partner))

    def b_far(j):
        b, o, at_b, at_o = axes(j)
        far = m4(b + 2)
        recv(b2[j][0], G.at[j, far, c, pl.ds(0, 2)])
        recv(b2[j][1], G.at[j, far, c, pl.ds(2, 2)])
        ds[j].append(send(G.at[j, far, c], G.at[j, far, c], partner))

    def core_done(j, ks):
        b = x if j < 2 else y
        for k in ks:
            recv(ds[j][k], G.at[j, m4(b + (0, -1, 1, 2)[k]), pc])

    for d in range(1, 8):
        recv(mz[d - 1], MZ.at[zidx(m8(z - d))])
    MC[c] = jnp.zeros((16, 128), F32)
    for h in range(4):
        MC[c, h : h + 1] = MZ[h, 0:1] + MZ[4 + h, 0:1]
    MC[c, 8:12] = MZ[zh, 4:8]
    MC[c, 12:16] = MZ[4 + zh, 4:8]
    mc = send(MC.at[c], MC.at[c], partner)
    z_done(0)
    z_done(2)
    recv(mc, MC.at[pc])
    MX[x] = jnp.zeros((24, 128), F32)
    MX[x, 0:8] = MC[0, 0:8] + MC[1, 0:8]
    MX[x, 8:16] = MC[0, 8:16]
    MX[x, 16:24] = MC[1, 8:16]
    mx = [send(MX.at[x], MX.at[x], at_x(d)) for d in (1, 2, 3)]
    z_done(1)
    z_done(3)
    for d in (1, 2, 3):
        recv(mx[d - 1], MX.at[m4(x - d)])
    MY[y] = MX[0, 0:8] + MX[1, 0:8] + MX[2, 0:8] + MX[3, 0:8]
    my = [send(MY.at[y], MY.at[y], at_y(d)) for d in (1, 2, 3)]
    o_far(0)
    o_near(1)
    o_far(2)
    o_near(3)
    o_far(1)
    o_far(3)
    for d in (1, 2, 3):
        recv(my[d - 1], MY.at[m4(y - d)])
    lane1 = lane_iota((8, 128))
    for yy in range(4):
        sums = MY[yy]
        inv = lax.rsqrt(jnp.where(lane1 < 32, sums / DT, sums / DS) + EPS)
        for h in range(4):
            wide = jnp.broadcast_to(inv[h : h + 1], (32, 128))
            base = (yy * 4 + h) * 32
            INVT[base : base + 32, :] = jnp.broadcast_to(jnp.sum(jnp.where(lane == sub, wide, 0.0), axis=1, keepdims=True), (32, 128))
            INVS[base : base + 32, :] = jnp.broadcast_to(jnp.sum(jnp.where(lane == sub + 32, wide, 0.0), axis=1, keepdims=True), (32, 128))
    sub2, lane2 = row_iota((128, 128)), lane_iota((128, 128))
    for blk in range(4):
        wide = jnp.broadcast_to(lab[blk : blk + 1, :].astype(F32), (128, 128))
        LAB[blk * 128 : blk * 128 + 128, :] = jnp.broadcast_to(jnp.sum(jnp.where(lane2 == sub2, wide, 0.0), axis=1, keepdims=True), (128, 128))
    lax.fori_loop(0, 16, wait_heads, 0)

    def teacher_block(x_):
        def norm(u, _):
            zl_, c_ = u // 2, u % 2
            for j in range(2):
                gain = MX[x_, pl.ds(8 + c_ * 8 + zl_ * 4 + j, 1)]
                for o_ in range(4):
                    rows = G[j, x_, c_, o_, pl.ds(zl_ * 4, 4)].reshape(128, 128).astype(F32)
                    r = rows * INVT[o_ * 128 : o_ * 128 + 128, :] * gain
                    NT[u, o_ * 128 : o_ * 128 + 128, j * 128 : j * 128 + 128] = r.astype(BF16)
            return 0

        lax.fori_loop(0, 4, norm, 0)

        def mul(n, _):
            cols = pl.ds(pl.multiple_of(n * 256, 256), 256)
            lt = jnp.concatenate([NT[u] for u in range(4)], axis=1)
            rt = jnp.concatenate([TA[x_ * 4 + u, :, cols] for u in range(4)], axis=0)
            accT[:, cols] += jnp.dot(lt, rt, preferred_element_type=F32)
            return 0

        lax.fori_loop(0, 2, mul, 0)

    def student_norm(y_):
        tok = pl.ds(pl.multiple_of(y_ * 128, 128), 128)

        def norm(v, _):
            x_, zl_, c_ = v // 4, (v // 2) % 2, v % 2
            for j in range(2):
                gain = MX[x_, pl.ds(8 + c_ * 8 + zl_ * 4 + 2 + j, 1)]
                rows = G[2 + j, y_, c_, x_, pl.ds(zl_ * 4, 4)].reshape(128, 128).astype(F32)
                inv = INVS[tok, :]
                if j == 0:
                    inv = jnp.where(lane2 < 32, INVT[tok, :], inv)
                NS[v, tok, j * 128 : j * 128 + 128] = (rows * inv * gain).astype(BF16)
            return 0

        lax.fori_loop(0, 16, norm, 0)

    def student_block(y_):
        tok = pl.ds(pl.multiple_of(y_ * 128, 128), 128)

        def mul(q, _):
            ls = jnp.concatenate([NS[q * 4 + u, tok, :] for u in range(4)], axis=1)
            rs = jnp.concatenate([SP[q * 4 + u] for u in range(4)], axis=0)
            lb = jnp.concatenate([NS[q * 4 + u, tok, 0:128] for u in range(4)], axis=1)
            rb = jnp.concatenate([TB[q * 4 + u] for u in range(4)], axis=0)
            accS[tok, :] += jnp.dot(ls, rs, preferred_element_type=F32)
            accT[tok, :] += jnp.dot(lb, rb, preferred_element_type=F32)
            return 0

        lax.fori_loop(0, 4, mul, 0)

    def flip(v, _):
        SPT[:, pl.ds(pl.multiple_of(v * 256, 256), 256)] = jnp.transpose(SP[v])
        return 0

    lax.fori_loop(0, 8, flip, 0)
    b_near(0)
    b_near(2)
    for j in range(4):
        core_done(j, (0,))
    teacher_block(x)
    b_near(1)
    b_near(3)
    student_norm(y)
    student_block(y)
    lax.fori_loop(8, 16, flip, 0)
    b_far(0)
    b_far(2)
    for j in range(4):
        core_done(j, (1, 2))

    def teacher_near(i, _):
        teacher_block(m4(x - 1 + 2 * i))
        return 0

    def student_near(i, _):
        y_ = m4(y - 1 + 2 * i)
        student_norm(y_)
        student_block(y_)
        return 0

    lax.fori_loop(0, 2, teacher_near, 0)
    b_far(1)
    b_far(3)
    lax.fori_loop(0, 2, student_near, 0)
    for j in range(4):
        core_done(j, (3,))
    teacher_block(m4(x + 2))
    student_norm(m4(y + 2))
    student_block(m4(y + 2))

    first = (dp * 16 + vo) * 512

    def stats(i, _):
        rows = pl.ds(pl.multiple_of(i * 64, 64), 64)
        tl = CAP * jnp.tanh(accT[rows, :] / CAP)
        sl = CAP * jnp.tanh(accS[rows, :] / CAP)
        et, es = jnp.exp(tl), jnp.exp(sl)
        want = LAB[rows, 0:1]
        hit = (lane_iota((64, 512)) + first).astype(F32) == want
        picked = jnp.sum(jnp.where(hit, sl, 0.0), axis=1, keepdims=True)
        cross = jnp.sum(et * (tl - sl), axis=1, keepdims=True)
        tot_t = jnp.sum(et, axis=1, keepdims=True)
        tot_s = jnp.sum(es, axis=1, keepdims=True)
        ln = lane_iota((64, 128))
        ST[rows, :] = jnp.where(ln == 0, tot_t, jnp.where(ln == 1, tot_s, jnp.where(ln == 2, cross, jnp.where(ln == 3, picked, 0.0))))
        accZ[rows, :] = accS[rows, :]
        slope = SCALE * (1.0 - (sl / CAP) ** 2)
        accA[rows, :] = 1.5 * es * slope
        accT[rows, :] = et * slope
        accS[rows, :] = jnp.where(hit, 0.5 * slope, 0.0)
        return 0

    lax.fori_loop(0, 8, stats, 0)
    for blk in range(4):
        t = jnp.transpose(ST[blk * 128 : blk * 128 + 128, :])
        for q in range(4):
            TC[c, q * 4 + blk : q * 4 + blk + 1] = t[q : q + 1]
    n = send(TC.at[c], TC.at[c], partner)
    recv(n, TC.at[pc])
    TX[x] = TC[0] + TC[1]
    ns = [send(TX.at[x], TX.at[x], at_x(d)) for d in (1, 2, 3)]
    for d in (1, 2, 3):
        recv(ns[d - 1], TX.at[m4(x - d)])
    TY[y] = TX[0] + TX[1] + TX[2] + TX[3]
    ns = [send(TY.at[y], TY.at[y], at_y(d)) for d in (1, 2, 3)]
    for d in (1, 2, 3):
        recv(ns[d - 1], TY.at[m4(y - d)])
    TZ[zz] = TY[0] + TY[1] + TY[2] + TY[3]
    ns = [send(TZ.at[zz], TZ.at[zz], at_z(d)) for d in range(1, 8)]
    for d in range(1, 8):
        recv(ns[d - 1], TZ.at[zidx(m8(z - d))])
    total = TZ[0]
    for i in range(1, 8):
        total = total + TZ[i]
    tt, ts, cr, pk = total[0:4], total[4:8], total[8:12], total[12:16]
    ls = jnp.log(ts)
    token_loss = cr / tt - jnp.log(tt) + ls + 0.5 * (ls - pk)
    loss_o[...] = jnp.sum(jnp.sum(token_loss, axis=1, keepdims=True), axis=0, keepdims=True) / TOKENS
    rec = 1.0 / total[0:8]
    SQ[...] = jnp.zeros_like(SQ)
    for blk in range(4):
        SQ[0:1, :] = rec[blk : blk + 1]
        SQ[1:2, :] = rec[4 + blk : 5 + blk]
        ST[blk * 128 : blk * 128 + 128, :] = jnp.transpose(SQ[...])

    def grads(i, _):
        rows = pl.ds(pl.multiple_of(i * 64, 64), 64)
        g = (accA[rows, :] * ST[rows, 1:2] - accT[rows, :] * ST[rows, 0:1] - accS[rows, :]).astype(BF16)
        gl[rows, :] = g
        dots = jnp.sum(g.astype(F32) * accZ[rows, :], axis=1, keepdims=True)
        LAB[rows, :] = jnp.broadcast_to(dots, (64, 128))
        return 0

    lax.fori_loop(0, 8, grads, 0)

    def as_row(column):
        return jnp.sum(jnp.where(lane2 == sub2, column, 0.0), axis=0, keepdims=True)

    def partial(v):
        return jnp.dot(gl[...], SPT[:, pl.ds(pl.multiple_of(v * 256, 256), 256)], preferred_element_type=F32).astype(BF16)

    def share(dst, x_, c_):
        def one(zl_, _):
            out = partial(x_ * 4 + zl_ * 2 + c_)
            for y_ in range(4):
                part = out[y_ * 128 : y_ * 128 + 128]
                dst[0, x_, y_, pl.ds(zl_ * 4, 4)] = part[:, 0:128].reshape(4, 32, 128)
                dst[1, y_, x_, pl.ds(zl_ * 4, 4)] = part[:, 128:256].reshape(4, 32, 128)
            return 0

        lax.fori_loop(0, 2, one, 0)

    order = [m4(x + 2), m4(x + 1), m4(x - 1), x]
    ps = []
    for x_ in order:
        share(PS, x_, pc)
        ps.append((send(PS.at[0, x_], PR.at[0, x_], partner), send(PS.at[1, :, x_], PR.at[1, :, x_], partner)))
    r1 = {}
    for i, x_ in enumerate(order):
        share(R, x_, c)
        recv(ps[i][0], PR.at[0, x_])
        for o_ in range(4):
            R[0, x_, o_] = (R[0, x_, o_].astype(F32) + PR[0, x_, o_].astype(F32)).astype(BF16)
        recv(ps[i][1], PR.at[1, :, x_])
        for b_ in range(4):
            R[1, b_, x_] = (R[1, b_, x_].astype(F32) + PR[1, b_, x_].astype(F32)).astype(BF16)
        if i == 0:
            r1[0] = (
                send(R.at[0, x_, pl.ds(0, 2)], RH.at[0, 0], at_x(1)),
                send(R.at[0, x_, pl.ds(2, 2)], RH.at[0, 1], at_x(-1)),
            )
    far = m4(y + 2)
    r1[1] = (
        send(R.at[1, far, pl.ds(0, 2)], RH.at[1, 0], at_y(1)),
        send(R.at[1, far, pl.ds(2, 2)], RH.at[1, 1], at_y(-1)),
    )

    def head_grad(v, _):
        out = lax.dot_general(NS[v], gl[...], (((0,), (0,)), ((), ())), preferred_element_type=F32)
        hg_o[pl.ds(pl.multiple_of(v * WS, 16), WS), :] = out[32:256].astype(BF16)
        sums = jnp.sum(out * SP[v].astype(F32), axis=1, keepdims=True)
        for h in range(2):
            GI[c, pl.ds(2 * v + h, 1)] = as_row(sums[h * 128 : h * 128 + 128])
        return 0

    GI[c, 32:40] = jnp.zeros((8, 128), F32)
    for blk in range(4):
        GI[c, 32 + blk : 33 + blk] = as_row(LAB[blk * 128 : blk * 128 + 128, :])
    lax.fori_loop(0, 8, head_grad, 0)
    r2 = {}
    for k in range(2):
        b = x if k == 0 else y
        at_b = at_x if k == 0 else at_y
        recv(r1[k][0], RH.at[k, 0])
        for o_ in range(2):
            R[k, m4(b + 1), o_] = (R[k, m4(b + 1), o_].astype(F32) + RH[k, 0, o_].astype(F32)).astype(BF16)
        n0 = send(R.at[k, m4(b + 1)], RB.at[k, 0], at_b(1))
        recv(r1[k][1], RH.at[k, 1])
        for o_ in range(2):
            R[k, m4(b - 1), 2 + o_] = (R[k, m4(b - 1), 2 + o_].astype(F32) + RH[k, 1, o_].astype(F32)).astype(BF16)
        n1 = send(R.at[k, m4(b - 1)], RB.at[k, 1], at_b(-1))
        r2[k] = (n0, n1)
    lax.fori_loop(8, 16, head_grad, 0)
    gi = send(GI.at[c], GI.at[c], partner)
    recv(gi, GI.at[pc])
    for x_ in range(4):
        GX[x_, 0:8] = GI[0, 8 * x_ : 8 * x_ + 8] + GI[1, 8 * x_ : 8 * x_ + 8]
        GX[x_, 8:16] = GI[0, 32:40] + GI[1, 32:40]
    GXR[x] = GX[x]
    gx = [send(GX.at[m4(x + d)], GXR.at[x], at_x(d)) for d in (1, 2, 3)]
    r3 = {}
    for k in range(2):
        b, o = (x, y) if k == 0 else (y, x)
        at_o = at_y if k == 0 else at_x
        recv(r2[k][0], RB.at[k, 0])
        recv(r2[k][1], RB.at[k, 1])
        for o_ in range(4):
            Q[k, o_] = (R[k, b, o_].astype(F32) + RB[k, 0, o_].astype(F32) + RB[k, 1, o_].astype(F32)).astype(BF16)
        r3[k] = [send(Q.at[k, m4(o + d)], QR.at[k, d - 1], at_o(d)) for d in (1, 2, 3)]
    for d in (1, 2, 3):
        recv(gx[d - 1], GXR.at[m4(x - d)])
    GY[y] = GXR[0] + GXR[1] + GXR[2] + GXR[3]
    gy = [send(GY.at[y], GY.at[y], at_y(d)) for d in (1, 2, 3)]
    r4 = {}
    for k in range(2):
        o = y if k == 0 else x
        for d in (1, 2, 3):
            recv(r3[k][d - 1], QR.at[k, d - 1])
        W[k] = (Q[k, o].astype(F32) + QR[k, 0].astype(F32) + QR[k, 1].astype(F32) + QR[k, 2].astype(F32)).astype(BF16)
        r4[k] = [send(W.at[k, zidx(m8(z + d))], ZR.at[k, d - 1], at_z(d)) for d in range(1, 8)]
    for d in (1, 2, 3):
        recv(gy[d - 1], GY.at[m4(y - d)])
    GZ[zz] = GY[0] + GY[1] + GY[2] + GY[3]
    gz = [send(GZ.at[zz], GZ.at[zz], at_z(d)) for d in range(1, 8)]
    for k in range(2):
        for d in range(1, 8):
            recv(r4[k][d - 1], ZR.at[k, d - 1])
        got = W[k, zz].astype(F32)
        for d in range(7):
            got = got + ZR[k, d].astype(F32)
        NG[:, k * 128 : k * 128 + 128] = got

    own = pl.ds(pl.multiple_of(dp * 32, 32), 32)
    inv = INVS[own, 0:1]
    ng = NG[...]
    rows = AS[0:32, :]
    gain = AS[32:33, :]
    scaled = ng * gain
    for d in range(1, 8):
        recv(gz[d - 1], GZ.at[zidx(m8(z - d))])
    total = GZ[0]
    for i in range(1, 8):
        total = total + GZ[i]
    GT[...] = total
    wide = jnp.broadcast_to(GT[pl.ds(8 + y, 1)], (32, 128))
    inner = jnp.sum(jnp.where(lane == sub + zh * 32, wide, 0.0), axis=1, keepdims=True) / DS
    out = inv * scaled - rows * (inv * inv) * inner
    rows_o[...] = pltpu.roll(out, 224, 1)[:, 0:WS]
    at = (zl * 2 + c) * 2
    sums = jnp.concatenate([GT[pl.ds(at, 1)], GT[pl.ds(at + 1, 1)]], axis=1)
    sums = sums / jnp.where(lane_iota((1, 256)) < 32, 1.0, gain)
    gain_o[...] = pltpu.roll(jnp.broadcast_to(sums, (8, 256)), 224, 1)[0:1, 0:WS]
    for cp in sent:
        cp.wait_send()


def local(teacher_rows, student_rows, teacher_gain, student_gain, teacher_head, student_head, labels):
    vmem = pl.BlockSpec(memory_space=pltpu.VMEM)
    anyw = pl.BlockSpec(memory_space=pl.ANY)
    V = pltpu.VMEM
    loss, gain_grad, rows_grad, head_grad = pl.pallas_call(
        kernel,
        out_shape=(
            jax.ShapeDtypeStruct((1, 1), F32),
            jax.ShapeDtypeStruct((1, WS), F32),
            jax.ShapeDtypeStruct((32, WS), F32),
            jax.ShapeDtypeStruct((DS, 512), BF16),
        ),
        in_specs=[vmem, vmem, vmem, vmem, vmem, anyw, anyw],
        out_specs=(vmem, vmem, vmem, vmem),
        scratch_shapes=[
            V((4, 4, 2, 4, 8, 32, 128), BF16),
            V((16, 256, 512), BF16),
            V((16, 128, 512), BF16),
            V((16, 256, 512), BF16),
            V((512, 4096), BF16),
            V((512, 512), F32), V((512, 512), F32), V((512, 512), F32),
            V((4, 512, 256), BF16), V((16, 512, 256), BF16),
            V((512, 512), BF16),
            V((512, 512), F32),
            V((40, 384), F32), V((40, 256), F32),
            V((512, 128), F32), V((512, 128), F32), V((512, 128), F32), V((512, 128), F32),
            V((128, 128), F32),
            V((8, 8, 128), F32), V((2, 16, 128), F32), V((4, 24, 128), F32), V((4, 8, 128), F32),
            V((2, 16, 128), F32), V((4, 16, 128), F32), V((4, 16, 128), F32), V((8, 16, 128), F32),
            V((2, 4, 4, 8, 32, 128), BF16), V((2, 4, 4, 8, 32, 128), BF16), V((2, 4, 4, 8, 32, 128), BF16),
            V((2, 2, 2, 8, 32, 128), BF16), V((2, 2, 4, 8, 32, 128), BF16),
            V((2, 4, 8, 32, 128), BF16), V((2, 3, 8, 32, 128), BF16),
            V((2, 8, 32, 128), BF16), V((2, 7, 32, 128), BF16),
            V((32, 256), F32),
            V((2, 40, 128), F32), V((4, 16, 128), F32), V((4, 16, 128), F32),
            V((4, 16, 128), F32), V((8, 16, 128), F32), V((16, 128), F32),
            pltpu.SemaphoreType.DMA((3, 16)),
            pltpu.SemaphoreType.DMA((NSEM,)),
            pltpu.SemaphoreType.DMA((NSEM,)),
        ],
        compiler_params=pltpu.CompilerParams(
            collective_id=0, has_side_effects=True, vmem_limit_bytes=47 << 20
        ),
    )(
        teacher_rows, student_rows, teacher_gain, student_gain,
        labels.reshape(4, 128), teacher_head, student_head,
    )
    return loss.reshape(()), head_grad, gain_grad.reshape(WS), rows_grad


def solution(mesh):
    in_specs = (
        P("dp", "vocab"),
        P("dp", "vocab"),
        P("vocab"),
        P("vocab"),
        P(None, ("dp", "vocab")),
        P(None, ("dp", "vocab")),
        P(),
    )
    out_specs = (P(), P(None, ("dp", "vocab")), P("vocab"), P("dp", "vocab"))
    return jax.shard_map(local, mesh=mesh, in_specs=in_specs, out_specs=out_specs, check_vma=False)
```

profile of v0, /device:TPU:32, one launch (start us, length us, event | category | flops | bytes accessed | tf_op | source)
XLA Modules:
  0.0 111.4 jit_solution(285825368803569856)
XLA Ops:
  0.6 0.0 copy-start.1
  0.6 0.7 copy-done.1
  1.4 0.0 copy-start.2
  1.4 0.7 copy-done.2
  2.1 0.0 copy-start.3
  2.1 0.7 copy-done.3
  2.8 0.0 copy-start.4
  2.8 0.7 copy-done.4
  3.5 0.0 copy-start.5
  3.5 0.7 copy-done.5
  4.1 98.5 %shard_map.102 = (f32[1,1]{1,0:T(1,128)}, f32[1,224]{1,0:T(1,128)S(1)}, f32[32,224]{1,0:T(8,128)S(1)}, bf16[3584,512]{1,0:T(8,128)(2,1)S(1)}) custom-call(bf16[32,288]{1,0:T(8,128)(2,1)S(1)} %copy-done.1, bf16[32,224]{1,0:T(8,128)(2,1)S(1)} %copy-done.2, bf16[288]{0:T(512)(128)(2,1)S(1)} %copy-done.4, bf16[224]{0:T(256)(128)(2,1)S(1)} %copy-done.5, ...), custom_call_target="tpu_custom_call" | custom-call | tf_op jit(solution)/shard_map/pallas_call | solution.py:549
  102.6 0.0 copy-start
  102.6 1.8 %copy-done = bf16[3584,512]{1,0:T(8,128)(2,1)} copy-done((bf16[3584,512]{1,0:T(8,128)(2,1)}, bf16[3584,512]{1,0:T(8,128)(2,1)S(1)}, u32[]{:S(2)}) %copy-start) | copy-done | bytes 3670040
  105.0 4.1 %copy.16 = bf16[3584,512]{1,0:T(8,128)(2,1)} copy(bf16[3584,512]{1,0:T(8,128)(2,1)} %copy-done) | data formatting | bytes 7340032
  109.1 0.6 copy.17
  109.7 0.6 copy.18
Async XLA Ops:
  0.6 0.7 copy-start.1
  1.4 0.7 copy-start.2
  2.1 0.7 copy-start.3
  2.8 0.7 copy-start.4
  3.5 0.7 copy-start.5
  102.6 1.8 %copy-start = (bf16[3584,512]{1,0:T(8,128)(2,1)}, bf16[3584,512]{1,0:T(8,128)(2,1)S(1)}, u32[]{:S(2)}) copy-start(bf16[3584,512]{1,0:T(8,128)(2,1)S(1)} %get-tuple-element.17) | copy-start | bytes 11010052
where the time goes:
time: 112 us; the launch traced here: 111 us
  Pallas kernels  98.5 us (88%)
  local copies, waits for them, and re-layouts  10.5 us (9%)
  between operations  2.37 us (2%)
    pallas_call x1, Pallas kernels, local(): pl.pallas_call(kernel, out_shape=(jax.ShapeDtypeStruct((1, 1), F32), jax....  98.5 us
    unnamed x15, local copies, waits for them, and re-layouts  10.5 us

commit v1 on v0

--- a/solution.py
+++ b/solution.py
@@ -30,14 +30,14 @@
 
 
 def kernel(
-    tr, sr, tg, sg, lab, th, sh,
+    tr_h, sr_h, tg_h, sg_h, lab_h, th, sh,
     loss_o, gain_o, rows_o, hg_o,
     G, TA, TB, SP, SPT, accT, accS, accA, NT, NS, gl, accZ,
     AT, AS, INVT, INVS, ST, LAB, SQ,
     MZ, MC, MX, MY, TC, TX, TY, TZ,
     PS, PR, R, RH, RB, Q, QR, W, ZR, NG,
     GI, GX, GXR, GY, GZ, GT,
-    hsem, ssem, rsem,
+    tr, sr, tg, sg, lab, isem, hsem, ssem, rsem,
 ):
     dp = lax.axis_index("dp")
     vo = lax.axis_index("vocab")
@@ -103,6 +103,12 @@
             cp.wait()
         return 0
 
+    own_copies = [
+        pltpu.make_async_copy(src, dst, isem.at[i])
+        for i, (src, dst) in enumerate(((tr_h, tr), (sr_h, sr), (tg_h, tg), (sg_h, sg), (lab_h, lab)))
+    ]
+    for cp in own_copies:
+        cp.start()
     barrier = pltpu.get_barrier_semaphore()
     others = [partner] + [at_x(d) for d in (1, 2, 3)] + [at_y(d) for d in (1, 2, 3)] + [at_z(d) for d in range(1, 8)]
     for d in others:
@@ -110,6 +116,8 @@
 
     AT[...] = jnp.zeros_like(AT)
     AS[...] = jnp.zeros_like(AS)
+    for cp in own_copies:
+        cp.wait()
     AT[0:32, 0:WT] = tr[...].astype(F32)
     AS[0:32, 0:WS] = sr[...].astype(F32)
     AT[32:40, 0:WT] = jnp.broadcast_to(tg[...].astype(F32).reshape(1, WT), (8, WT))
@@ -133,10 +141,14 @@
 
     mz = [send(MZ.at[zz], MZ.at[zz], at_z(d)) for d in range(1, 8)]
     zs = {}
-    for j in (0, 2, 1, 3):
+
+    def z_send(j):
         b, o = (x, y) if j < 2 else (y, x)
         piece = G.at[j, b, c, o, zz]
         zs[j] = [send(piece, piece, at_z(d)) for d in range(1, 8)]
+
+    z_send(0)
+    z_send(2)
 
     def start_heads(v, _):
         for cp in head_copies(v):
@@ -209,6 +221,10 @@
         for k in ks:
             recv(ds[j][k], G.at[j, m4(b + (0, -1, 1, 2)[k]), pc])
 
+    z_done(0)
+    z_done(2)
+    z_send(1)
+    z_send(3)
     for d in range(1, 8):
         recv(mz[d - 1], MZ.at[zidx(m8(z - d))])
     MC[c] = jnp.zeros((16, 128), F32)
@@ -217,23 +233,21 @@
     MC[c, 8:12] = MZ[zh, 4:8]
     MC[c, 12:16] = MZ[4 + zh, 4:8]
     mc = send(MC.at[c], MC.at[c], partner)
-    z_done(0)
-    z_done(2)
     recv(mc, MC.at[pc])
     MX[x] = jnp.zeros((24, 128), F32)
     MX[x, 0:8] = MC[0, 0:8] + MC[1, 0:8]
     MX[x, 8:16] = MC[0, 8:16]
     MX[x, 16:24] = MC[1, 8:16]
     mx = [send(MX.at[x], MX.at[x], at_x(d)) for d in (1, 2, 3)]
+    o_far(0)
+    o_far(2)
     z_done(1)
     z_done(3)
     for d in (1, 2, 3):
         recv(mx[d - 1], MX.at[m4(x - d)])
     MY[y] = MX[0, 0:8] + MX[1, 0:8] + MX[2, 0:8] + MX[3, 0:8]
     my = [send(MY.at[y], MY.at[y], at_y(d)) for d in (1, 2, 3)]
-    o_far(0)
     o_near(1)
-    o_far(2)
     o_near(3)
     o_far(1)
     o_far(3)
@@ -292,16 +306,22 @@
 
         lax.fori_loop(0, 16, norm, 0)
 
-    def student_block(y_):
-        tok = pl.ds(pl.multiple_of(y_ * 128, 128), 128)
+    def student_block(ys):
+        toks = [pl.ds(pl.multiple_of(y_ * 128, 128), 128) for y_ in ys]
+
+        def lhs(q, width):
+            return jnp.concatenate(
+                [jnp.concatenate([NS[q * 4 + u, tok, 0:width] for u in range(4)], axis=1) for tok in toks], axis=0
+            )
 
         def mul(q, _):
-            ls = jnp.concatenate([NS[q * 4 + u, tok, :] for u in range(4)], axis=1)
             rs = jnp.concatenate([SP[q * 4 + u] for u in range(4)], axis=0)
-            lb = jnp.concatenate([NS[q * 4 + u, tok, 0:128] for u in range(4)], axis=1)
             rb = jnp.concatenate([TB[q * 4 + u] for u in range(4)], axis=0)
-            accS[tok, :] += jnp.dot(ls, rs, preferred_element_type=F32)
-            accT[tok, :] += jnp.dot(lb, rb, preferred_element_type=F32)
+            s_part = jnp.dot(lhs(q, 256), rs, preferred_element_type=F32)
+            t_part = jnp.dot(lhs(q, 128), rb, preferred_element_type=F32)
+            for i, tok in enumerate(toks):
+                accS[tok, :] += s_part[i * 128 : i * 128 + 128]
+                accT[tok, :] += t_part[i * 128 : i * 128 + 128]
             return 0
 
         lax.fori_loop(0, 4, mul, 0)
@@ -310,41 +330,41 @@
         SPT[:, pl.ds(pl.multiple_of(v * 256, 256), 256)] = jnp.transpose(SP[v])
         return 0
 
-    lax.fori_loop(0, 8, flip, 0)
-    b_near(0)
-    b_near(2)
     for j in range(4):
         core_done(j, (0,))
     teacher_block(x)
+    student_norm(y)
+    b_near(0)
+    b_near(2)
+    student_block([y])
     b_near(1)
     b_near(3)
-    student_norm(y)
-    student_block(y)
-    lax.fori_loop(8, 16, flip, 0)
+    lax.fori_loop(0, 16, flip, 0)
+    for j in (0, 1):
+        core_done(j, (1, 2))
+
+    def teacher_near(i, _):
+        teacher_block(m4(x - 1 + 2 * i))
+        return 0
+
+    def student_near(i, _):
+        student_norm(m4(y - 1 + 2 * i))
+        return 0
+
+    lax.fori_loop(0, 2, teacher_near, 0)
     b_far(0)
     b_far(2)
-    for j in range(4):
+    for j in (2, 3):
         core_done(j, (1, 2))
-
-    def teacher_near(i, _):
-        teacher_block(m4(x - 1 + 2 * i))
-        return 0
-
-    def student_near(i, _):
-        y_ = m4(y - 1 + 2 * i)
-        student_norm(y_)
-        student_block(y_)
-        return 0
-
-    lax.fori_loop(0, 2, teacher_near, 0)
+    lax.fori_loop(0, 2, student_near, 0)
     b_far(1)
     b_far(3)
-    lax.fori_loop(0, 2, student_near, 0)
+    student_block([m4(y - 1), m4(y + 1)])
     for j in range(4):
         core_done(j, (3,))
     teacher_block(m4(x + 2))
     student_norm(m4(y + 2))
-    student_block(m4(y + 2))
+    student_block([m4(y + 2)])
 
     first = (dp * 16 + vo) * 512
 
@@ -542,9 +562,21 @@
         cp.wait_send()
 
 
+def hand_over(gain_i, rows_i, hg_i, gain_o, rows_o, hg_o, sem):
+    copies = [pltpu.make_async_copy(gain_i, gain_o, sem.at[4]), pltpu.make_async_copy(rows_i, rows_o, sem.at[5])]
+    for i in range(4):
+        part = pl.ds(i * 896, 896)
+        copies.append(pltpu.make_async_copy(hg_i.at[part], hg_o.at[part], sem.at[i]))
+    for cp in copies:
+        cp.start()
+    for cp in copies:
+        cp.wait()
+
+
 def local(teacher_rows, student_rows, teacher_gain, student_gain, teacher_head, student_head, labels):
     vmem = pl.BlockSpec(memory_space=pltpu.VMEM)
     anyw = pl.BlockSpec(memory_space=pl.ANY)
+    hbm = pl.BlockSpec(memory_space=pltpu.HBM)
     V = pltpu.VMEM
     loss, gain_grad, rows_grad, head_grad = pl.pallas_call(
         kernel,
@@ -554,7 +586,7 @@
             jax.ShapeDtypeStruct((32, WS), F32),
             jax.ShapeDtypeStruct((DS, 512), BF16),
         ),
-        in_specs=[vmem, vmem, vmem, vmem, vmem, anyw, anyw],
+        in_specs=[hbm] * 7,
         out_specs=(vmem, vmem, vmem, vmem),
         scratch_shapes=[
             V((4, 4, 2, 4, 8, 32, 128), BF16),
@@ -578,6 +610,8 @@
             V((32, 256), F32),
             V((2, 40, 128), F32), V((4, 16, 128), F32), V((4, 16, 128), F32),
             V((4, 16, 128), F32), V((8, 16, 128), F32), V((16, 128), F32),
+            V((32, WT), BF16), V((32, WS), BF16), V((WT,), BF16), V((WS,), BF16), V((4, 128), jnp.int32),
+            pltpu.SemaphoreType.DMA((5,)),
             pltpu.SemaphoreType.DMA((3, 16)),
             pltpu.SemaphoreType.DMA((NSEM,)),
             pltpu.SemaphoreType.DMA((NSEM,)),
@@ -589,6 +623,18 @@
         teacher_rows, student_rows, teacher_gain, student_gain,
         labels.reshape(4, 128), teacher_head, student_head,
     )
+    gain_grad, rows_grad, head_grad = pl.pallas_call(
+        hand_over,
+        out_shape=(
+            jax.ShapeDtypeStruct((1, WS), F32),
+            jax.ShapeDtypeStruct((32, WS), F32),
+            jax.ShapeDtypeStruct((DS, 512), BF16),
+        ),
+        in_specs=[anyw] * 3,
+        out_specs=(hbm, hbm, hbm),
+        scratch_shapes=[pltpu.SemaphoreType.DMA((6,))],
+        compiler_params=pltpu.CompilerParams(vmem_limit_bytes=8 << 20),
+    )(gain_grad, rows_grad, head_grad)
     return loss.reshape(()), head_grad, gain_grad.reshape(WS), rows_grad
 
 

time: 112 us -> 104 us (0.929)
  local copies, waits for them, and re-layouts: 10.5 us -> 3.46 us
    unnamed x15 -> x10, local copies, waits for them, and re-layouts: 10.5 us -> 3.46 us
    pallas_call x1, Pallas kernels: 98.5 us -> 96.4 us  [local(): pl.pallas_call(kernel, out_shape=(jax.ShapeDtypeStruct((1, 1), F32), jax....]
    pallas_call x0 -> x1, Pallas kernels: none -> 1.9 us  [local(): pl.pallas_call(hand_over, out_shape=(jax.ShapeDtypeStruct((1, WS), F32),...]
where the time goes in v1:
time: 104 us
  Pallas kernels  98.3 us (95%)
  local copies, waits for them, and re-layouts  3.46 us (3%)
  between operations  2.47 us (2%)
    pallas_call x1, Pallas kernels, local(): pl.pallas_call(kernel, out_shape=(jax.ShapeDtypeStruct((1, 1), F32), jax....  96.4 us
    unnamed x10, local copies, waits for them, and re-layouts  3.46 us

profile of v1, /device:TPU:32, one launch (start us, length us, event | category | flops | bytes accessed | tf_op | source)
XLA Modules:
  0.0 104.2 jit_solution(17793832707941070155)
XLA Ops:
  0.6 0.0 copy-start
  0.6 0.7 copy-done
  1.4 0.0 copy-start.1
  1.4 0.7 copy-done.1
  2.1 0.0 copy-start.2
  2.1 0.7 copy-done.2
  2.8 0.0 copy-start.3
  2.8 0.7 copy-done.3
  3.5 0.0 copy-start.4
  3.5 0.7 copy-done.4
  4.1 96.4 %shard_map.102 = (f32[1,1]{1,0:T(1,128)}, f32[1,224]{1,0:T(1,128)S(1)}, f32[32,224]{1,0:T(8,128)S(1)}, bf16[3584,512]{1,0:T(8,128)(2,1)S(1)}) custom-call(bf16[32,288]{1,0:T(8,128)(2,1)S(1)} %copy-done, bf16[32,224]{1,0:T(8,128)(2,1)S(1)} %copy-done.1, bf16[288]{0:T(512)(128)(2,1)S(1)} %copy-done.3, bf16[224]{0:T(256)(128)(2,1)S(1)} %copy-done.4, ...), custom_call_target="tpu_custom_call" | custom-call | tf_op jit(solution)/shard_map/pallas_call | solution.py:581
  100.5 1.9 %shard_map.103 = (f32[1,224]{1,0:T(1,128)}, f32[32,224]{1,0:T(8,128)}, bf16[3584,512]{1,0:T(8,128)(2,1)}) custom-call(f32[1,224]{1,0:T(1,128)S(1)} %get-tuple-element.12.gain_i, f32[32,224]{1,0:T(8,128)S(1)} %get-tuple-element.13.rows_i, bf16[3584,512]{1,0:T(8,128)(2,1)S(1)} %get-tuple-element.14.hg_i), custom_call_target="tpu_custom_call" | custom-call | tf_op jit(solution)/shard_map/pallas_call | solution.py:626
Async XLA Ops:
  0.6 0.7 copy-start
  1.4 0.7 copy-start.1
  2.1 0.7 copy-start.2
  2.8 0.7 copy-start.3
  3.5 0.7 copy-start.4

commit v2 on v1

--- a/solution.py
+++ b/solution.py
@@ -18,7 +18,7 @@
 EPS = 1e-06
 WT = 288
 WS = 224
-NSEM = 160
+NSEM = 240
 
 
 def row_iota(shape):
@@ -454,6 +454,12 @@
         share(PS, x_, pc)
         ps.append((send(PS.at[0, x_], PR.at[0, x_], partner), send(PS.at[1, :, x_], PR.at[1, :, x_], partner)))
     r1 = {}
+    row_order = ((2, 0, 0), (-1, 1, 0), (1, 0, 1), (0, 1, 1))
+
+    def far_row(k, e, way, n):
+        b, o, at_b = (x, y, at_x) if k == 0 else (y, x, at_y)
+        r1[k, e] = send(R.at[k, m4(b + 2), m4(o + e)], RH.at[k, way, n], at_b(1 - 2 * way))
+
     for i, x_ in enumerate(order):
         share(R, x_, c)
         recv(ps[i][0], PR.at[0, x_])
@@ -463,15 +469,9 @@
         for b_ in range(4):
             R[1, b_, x_] = (R[1, b_, x_].astype(F32) + PR[1, b_, x_].astype(F32)).astype(BF16)
         if i == 0:
-            r1[0] = (
-                send(R.at[0, x_, pl.ds(0, 2)], RH.at[0, 0], at_x(1)),
-                send(R.at[0, x_, pl.ds(2, 2)], RH.at[0, 1], at_x(-1)),
-            )
-    far = m4(y + 2)
-    r1[1] = (
-        send(R.at[1, far, pl.ds(0, 2)], RH.at[1, 0], at_y(1)),
-        send(R.at[1, far, pl.ds(2, 2)], RH.at[1, 1], at_y(-1)),
-    )
+            for row in row_order:
+                far_row(0, *row)
+        far_row(1, *row_order[(0, 2, 1, 3)[i]])
 
     def head_grad(v, _):
         out = lax.dot_general(NS[v], gl[...], (((0,), (0,)), ((), ())), preferred_element_type=F32)
@@ -486,18 +486,17 @@
         GI[c, 32 + blk : 33 + blk] = as_row(LAB[blk * 128 : blk * 128 + 128, :])
     lax.fori_loop(0, 8, head_grad, 0)
     r2 = {}
-    for k in range(2):
-        b = x if k == 0 else y
-        at_b = at_x if k == 0 else at_y
-        recv(r1[k][0], RH.at[k, 0])
-        for o_ in range(2):
-            R[k, m4(b + 1), o_] = (R[k, m4(b + 1), o_].astype(F32) + RH[k, 0, o_].astype(F32)).astype(BF16)
-        n0 = send(R.at[k, m4(b + 1)], RB.at[k, 0], at_b(1))
-        recv(r1[k][1], RH.at[k, 1])
-        for o_ in range(2):
-            R[k, m4(b - 1), 2 + o_] = (R[k, m4(b - 1), 2 + o_].astype(F32) + RH[k, 1, o_].astype(F32)).astype(BF16)
-        n1 = send(R.at[k, m4(b - 1)], RB.at[k, 1], at_b(-1))
-        r2[k] = (n0, n1)
+    for i, (e, way, n) in enumerate(row_order):
+        for k in range(2):
+            b, o, at_b = (x, y, at_x) if k == 0 else (y, x, at_y)
+            r = m4(o + e)
+            recv(r1[k, e], RH.at[k, way, n])
+            near = m4(b + 1 - 2 * way)
+            R[k, near, r] = (R[k, near, r].astype(F32) + RH[k, way, n].astype(F32)).astype(BF16)
+            r2[k, e] = (
+                send(R.at[k, m4(b + 1), r], RB.at[k, 0, i], at_b(1)),
+                send(R.at[k, m4(b - 1), r], RB.at[k, 1, i], at_b(-1)),
+            )
     lax.fori_loop(8, 16, head_grad, 0)
     gi = send(GI.at[c], GI.at[c], partner)
     recv(gi, GI.at[pc])
@@ -507,14 +506,15 @@
     GXR[x] = GX[x]
     gx = [send(GX.at[m4(x + d)], GXR.at[x], at_x(d)) for d in (1, 2, 3)]
     r3 = {}
-    for k in range(2):
-        b, o = (x, y) if k == 0 else (y, x)
-        at_o = at_y if k == 0 else at_x
-        recv(r2[k][0], RB.at[k, 0])
-        recv(r2[k][1], RB.at[k, 1])
-        for o_ in range(4):
-            Q[k, o_] = (R[k, b, o_].astype(F32) + RB[k, 0, o_].astype(F32) + RB[k, 1, o_].astype(F32)).astype(BF16)
-        r3[k] = [send(Q.at[k, m4(o + d)], QR.at[k, d - 1], at_o(d)) for d in (1, 2, 3)]
+    for i, (e, way, n) in enumerate(row_order):
+        for k in range(2):
+            b, o, at_o = (x, y, at_y) if k == 0 else (y, x, at_x)
+            r = m4(o + e)
+            recv(r2[k, e][0], RB.at[k, 0, i])
+            recv(r2[k, e][1], RB.at[k, 1, i])
+            Q[k, r] = (R[k, b, r].astype(F32) + RB[k, 0, i].astype(F32) + RB[k, 1, i].astype(F32)).astype(BF16)
+            if e != 0:
+                r3[k, e % 4] = send(Q.at[k, r], QR.at[k, e % 4 - 1], at_o(e))
     for d in (1, 2, 3):
         recv(gx[d - 1], GXR.at[m4(x - d)])
     GY[y] = GXR[0] + GXR[1] + GXR[2] + GXR[3]
@@ -523,7 +523,7 @@
     for k in range(2):
         o = y if k == 0 else x
         for d in (1, 2, 3):
-            recv(r3[k][d - 1], QR.at[k, d - 1])
+            recv(r3[k, d], QR.at[k, d - 1])
         W[k] = (Q[k, o].astype(F32) + QR[k, 0].astype(F32) + QR[k, 1].astype(F32) + QR[k, 2].astype(F32)).astype(BF16)
         r4[k] = [send(W.at[k, zidx(m8(z + d))], ZR.at[k, d - 1], at_z(d)) for d in range(1, 8)]
     for d in (1, 2, 3):

time: 104 us -> 105 us (level)
  no operation moved by 1% of the time
where the time goes in v2:
time: 105 us; the launch traced here: 104 us
  Pallas kernels  98.4 us (94%)
  local copies, waits for them, and re-layouts  3.46 us (3%)
  between operations  2.47 us (2%)
    pallas_call x1, Pallas kernels, local(): pl.pallas_call(kernel, out_shape=(jax.ShapeDtypeStruct((1, 1), F32), jax....  96.5 us
    unnamed x10, local copies, waits for them, and re-layouts  3.46 us

profile of v2, /device:TPU:32, one launch (start us, length us, event | category | flops | bytes accessed | tf_op | source)
XLA Modules:
  0.0 104.3 jit_solution(2480446900833803143)
XLA Ops:
  0.6 0.0 copy-start
  0.6 0.7 copy-done
  1.4 0.0 copy-start.1
  1.4 0.7 copy-done.1
  2.1 0.0 copy-start.2
  2.1 0.7 copy-done.2
  2.8 0.0 copy-start.3
  2.8 0.7 copy-done.3
  3.5 0.0 copy-start.4
  3.5 0.7 copy-done.4
  4.1 96.5 %shard_map.102 = (f32[1,1]{1,0:T(1,128)}, f32[1,224]{1,0:T(1,128)S(1)}, f32[32,224]{1,0:T(8,128)S(1)}, bf16[3584,512]{1,0:T(8,128)(2,1)S(1)}) custom-call(bf16[32,288]{1,0:T(8,128)(2,1)S(1)} %copy-done, bf16[32,224]{1,0:T(8,128)(2,1)S(1)} %copy-done.1, bf16[288]{0:T(512)(128)(2,1)S(1)} %copy-done.3, bf16[224]{0:T(256)(128)(2,1)S(1)} %copy-done.4, ...), custom_call_target="tpu_custom_call" | custom-call | tf_op jit(solution)/shard_map/pallas_call | solution.py:581
  100.6 1.9 %shard_map.103 = (f32[1,224]{1,0:T(1,128)}, f32[32,224]{1,0:T(8,128)}, bf16[3584,512]{1,0:T(8,128)(2,1)}) custom-call(f32[1,224]{1,0:T(1,128)S(1)} %get-tuple-element.12.gain_i, f32[32,224]{1,0:T(8,128)S(1)} %get-tuple-element.13.rows_i, bf16[3584,512]{1,0:T(8,128)(2,1)S(1)} %get-tuple-element.14.hg_i), custom_call_target="tpu_custom_call" | custom-call | tf_op jit(solution)/shard_map/pallas_call | solution.py:626
Async XLA Ops:
  0.6 0.7 copy-start
  1.4 0.7 copy-start.1
  2.1 0.7 copy-start.2
  2.8 0.7 copy-start.3
  3.5 0.7 copy-start.4

commit v3 on v1

--- a/solution.py
+++ b/solution.py
@@ -339,7 +339,6 @@
     student_block([y])
     b_near(1)
     b_near(3)
-    lax.fori_loop(0, 16, flip, 0)
     for j in (0, 1):
         core_done(j, (1, 2))
 
@@ -397,10 +396,12 @@
     recv(n, TC.at[pc])
     TX[x] = TC[0] + TC[1]
     ns = [send(TX.at[x], TX.at[x], at_x(d)) for d in (1, 2, 3)]
+    lax.fori_loop(0, 8, flip, 0)
     for d in (1, 2, 3):
         recv(ns[d - 1], TX.at[m4(x - d)])
     TY[y] = TX[0] + TX[1] + TX[2] + TX[3]
     ns = [send(TY.at[y], TY.at[y], at_y(d)) for d in (1, 2, 3)]
+    lax.fori_loop(8, 16, flip, 0)
     for d in (1, 2, 3):
         recv(ns[d - 1], TY.at[m4(y - d)])
     TZ[zz] = TY[0] + TY[1] + TY[2] + TY[3]

time: 104 us -> 104 us (level)
  no operation moved by 1% of the time
where the time goes in v3:
time: 104 us
  Pallas kernels  97.9 us (94%)
  local copies, waits for them, and re-layouts  3.46 us (3%)
  between operations  2.47 us (2%)
    pallas_call x1, Pallas kernels, local(): pl.pallas_call(kernel, out_shape=(jax.ShapeDtypeStruct((1, 1), F32), jax....  96 us
    unnamed x10, local copies, waits for them, and re-layouts  3.46 us

profile of v3, /device:TPU:32, one launch (start us, length us, event | category | flops | bytes accessed | tf_op | source)
XLA Modules:
  0.0 103.8 jit_solution(7299486530185843662)
XLA Ops:
  0.6 0.0 copy-start
  0.6 0.7 copy-done
  1.4 0.0 copy-start.1
  1.4 0.7 copy-done.1
  2.1 0.0 copy-start.2
  2.1 0.7 copy-done.2
  2.8 0.0 copy-start.3
  2.8 0.7 copy-done.3
  3.5 0.0 copy-start.4
  3.5 0.7 copy-done.4
  4.1 96.0 %shard_map.102 = (f32[1,1]{1,0:T(1,128)}, f32[1,224]{1,0:T(1,128)S(1)}, f32[32,224]{1,0:T(8,128)S(1)}, bf16[3584,512]{1,0:T(8,128)(2,1)S(1)}) custom-call(bf16[32,288]{1,0:T(8,128)(2,1)S(1)} %copy-done, bf16[32,224]{1,0:T(8,128)(2,1)S(1)} %copy-done.1, bf16[288]{0:T(512)(128)(2,1)S(1)} %copy-done.3, bf16[224]{0:T(256)(128)(2,1)S(1)} %copy-done.4, ...), custom_call_target="tpu_custom_call" | custom-call | tf_op jit(solution)/shard_map/pallas_call | solution.py:582
  100.1 1.9 %shard_map.103 = (f32[1,224]{1,0:T(1,128)}, f32[32,224]{1,0:T(8,128)}, bf16[3584,512]{1,0:T(8,128)(2,1)}) custom-call(f32[1,224]{1,0:T(1,128)S(1)} %get-tuple-element.12.gain_i, f32[32,224]{1,0:T(8,128)S(1)} %get-tuple-element.13.rows_i, bf16[3584,512]{1,0:T(8,128)(2,1)S(1)} %get-tuple-element.14.hg_i), custom_call_target="tpu_custom_call" | custom-call | tf_op jit(solution)/shard_map/pallas_call | solution.py:627
Async XLA Ops:
  0.6 0.7 copy-start
  1.4 0.7 copy-start.1
  2.1 0.7 copy-start.2
  2.8 0.7 copy-start.3
  3.5 0.7 copy-start.4

commit v4 on v3

--- a/solution.py
+++ b/solution.py
@@ -485,7 +485,7 @@
     GI[c, 32:40] = jnp.zeros((8, 128), F32)
     for blk in range(4):
         GI[c, 32 + blk : 33 + blk] = as_row(LAB[blk * 128 : blk * 128 + 128, :])
-    lax.fori_loop(0, 8, head_grad, 0)
+    lax.fori_loop(0, 10, head_grad, 0)
     r2 = {}
     for k in range(2):
         b = x if k == 0 else y
@@ -499,7 +499,7 @@
             R[k, m4(b - 1), 2 + o_] = (R[k, m4(b - 1), 2 + o_].astype(F32) + RH[k, 1, o_].astype(F32)).astype(BF16)
         n1 = send(R.at[k, m4(b - 1)], RB.at[k, 1], at_b(-1))
         r2[k] = (n0, n1)
-    lax.fori_loop(8, 16, head_grad, 0)
+    lax.fori_loop(10, 16, head_grad, 0)
     gi = send(GI.at[c], GI.at[c], partner)
     recv(gi, GI.at[pc])
     for x_ in range(4):

time: 104 us -> 105 us (level)
  no operation moved by 1% of the time
where the time goes in v4:
time: 105 us
  Pallas kernels  98.8 us (94%)
  local copies, waits for them, and re-layouts  3.46 us (3%)
  between operations  2.47 us (2%)
    pallas_call x1, Pallas kernels, local(): pl.pallas_call(kernel, out_shape=(jax.ShapeDtypeStruct((1, 1), F32), jax....  96.9 us
    unnamed x10, local copies, waits for them, and re-layouts  3.46 us

profile of v4, /device:TPU:32, one launch (start us, length us, event | category | flops | bytes accessed | tf_op | source)
XLA Modules:
  0.0 104.7 jit_solution(8636275489968797382)
XLA Ops:
  0.6 0.0 copy-start
  0.6 0.7 copy-done
  1.4 0.0 copy-start.1
  1.4 0.7 copy-done.1
  2.1 0.0 copy-start.2
  2.1 0.7 copy-done.2
  2.8 0.0 copy-start.3
  2.8 0.7 copy-done.3
  3.5 0.0 copy-start.4
  3.5 0.7 copy-done.4
  4.1 96.9 %shard_map.102 = (f32[1,1]{1,0:T(1,128)}, f32[1,224]{1,0:T(1,128)S(1)}, f32[32,224]{1,0:T(8,128)S(1)}, bf16[3584,512]{1,0:T(8,128)(2,1)S(1)}) custom-call(bf16[32,288]{1,0:T(8,128)(2,1)S(1)} %copy-done, bf16[32,224]{1,0:T(8,128)(2,1)S(1)} %copy-done.1, bf16[288]{0:T(512)(128)(2,1)S(1)} %copy-done.3, bf16[224]{0:T(256)(128)(2,1)S(1)} %copy-done.4, ...), custom_call_target="tpu_custom_call" | custom-call | tf_op jit(solution)/shard_map/pallas_call | solution.py:582
  101.0 1.9 %shard_map.103 = (f32[1,224]{1,0:T(1,128)}, f32[32,224]{1,0:T(8,128)}, bf16[3584,512]{1,0:T(8,128)(2,1)}) custom-call(f32[1,224]{1,0:T(1,128)S(1)} %get-tuple-element.12.gain_i, f32[32,224]{1,0:T(8,128)S(1)} %get-tuple-element.13.rows_i, bf16[3584,512]{1,0:T(8,128)(2,1)S(1)} %get-tuple-element.14.hg_i), custom_call_target="tpu_custom_call" | custom-call | tf_op jit(solution)/shard_map/pallas_call | solution.py:627
Async XLA Ops:
  0.6 0.7 copy-start
  1.4 0.7 copy-start.1
  2.1 0.7 copy-start.2
  2.8 0.7 copy-start.3
  3.5 0.7 copy-start.4
